TPU v7x, 512 devices: a whole 4x8x8 slice. The times are simulated.
512 devices in a mesh: island: 16 (over y, core), fsdp: 32 (over z, x).
Axes of the slice: x: 4, y: 8, z: 8, core: 2. Of those that a mesh axis runs over, the one named last changes fastest.
Arguments:
- delta: bfloat16 [16, 2048, 4096], P('island', 'fsdp'), may hold values from -6 to 6
- error: float32 [16, 2048, 4096], P('island', 'fsdp'), may hold values from -6 to 6
- param: bfloat16 [2048, 4096], P('fsdp'), may hold values from -6 to 6
- velocity: bfloat16 [2048, 4096], P('fsdp'), may hold values from -4 to 4
- piece_ids: int32 [32, 32, 16], P('fsdp'), may hold values from 0 to 2047, as said below
- piece_counts: int32 [32, 32], P('fsdp'), may hold values from 8 to 16, as said below
Outputs:
- new_error: float32 [16, 2048, 4096], P('island', 'fsdp')
- new_param: bfloat16 [2048, 4096], P('fsdp')
- new_velocity: bfloat16 [2048, 4096], P('fsdp')
- compressed: float32 [32, 32, 16, 128], P('fsdp')
Inputs may be any that keep to these rules, and one draw needn't show every extreme that they name: `piece_ids`: within one shard's lists all entries are distinct, entries past the count included; those are ignored. `piece_counts`: one owner receives exactly 16 live entries from every shard.
All inputs are finite; a program needn't handle non-finite values.
Results may differ from a plain program's by a relative error of at most 0.001.
Values sent between devices are 32-bit elements; how exact they have to be, the bound alone decides.
A program may use at most 64 MiB of HBM per device.

v0:
```python
import jax
import jax.numpy as jnp
from jax import lax
from jax.sharding import PartitionSpec as P

decay_rate = 0.9
outer_rate = 0.7
nesterov = 0.9
eps_value = 1e-06


def cosine_table(side):
    freq = jnp.arange(side, dtype=jnp.int32)[:, None].astype(jnp.float32)
    place = jnp.arange(side, dtype=jnp.int32)[None, :].astype(jnp.float32)
    scale = jnp.where(freq == 0.0, jnp.sqrt(1.0 / side), jnp.sqrt(2.0 / side))
    return scale * jnp.cos(jnp.pi * (2.0 * place + 1.0) * freq / (2.0 * side))


def transform(field, table, column_table):
    rows, width = field.shape
    side = table.shape[0]
    right = jnp.dot(field.reshape(-1, 128), column_table, precision=lax.Precision.HIGHEST)
    right = right.reshape(rows // side, side, width // 128, 128)
    left = jnp.einsum("kn,rnqj->rqkj", table, right, precision=lax.Precision.HIGHEST)
    return left.reshape(-1, 128)


def inverse(pieces, table, column_table, rows, width):
    side = table.shape[0]
    blocks = pieces.reshape(rows // side, width // 128, side, 128)
    left = jnp.einsum("kn,rqkj->rnqj", table, blocks, precision=lax.Precision.HIGHEST)
    back = jnp.dot(left.reshape(-1, 128), column_table.T, precision=lax.Precision.HIGHEST)
    return back.reshape(rows, width)


def normalize(values):
    return values / jnp.sqrt(jnp.mean(values * values, axis=-1, keepdims=True) + eps_value)


def island_norm(pieces):
    total = lax.psum(pieces, "island")
    return normalize(total)


def shards(delta, error, param, velocity, piece_ids, piece_counts):
    rows, width = param.shape
    table = cosine_table(64)
    column_table = jnp.kron(jnp.eye(2, dtype=jnp.float32), table.T)
    momentum = decay_rate * error[0] + delta[0].astype(jnp.float32)
    coefficients = transform(momentum, table, column_table)
    piece_list = piece_ids[0]
    owners, slots = piece_list.shape
    slot_index = jnp.arange(slots, dtype=jnp.int32)[None, :]
    active = (slot_index < piece_counts[0][:, None]).astype(jnp.float32)
    chosen = coefficients[piece_list] * active[..., None]
    flat_ids = piece_list.reshape(-1)
    arrived = lax.all_to_all(chosen, "fsdp", split_axis=0, concat_axis=0, tiled=True)
    compressed = island_norm(arrived)
    returned = lax.all_to_all(compressed, "fsdp", split_axis=0, concat_axis=0, tiled=True)
    kept_mask = (
        jnp.zeros((coefficients.shape[0],), jnp.float32).at[flat_ids].set(active.reshape(-1))
    )
    new_error = momentum - inverse(
        coefficients * kept_mask[:, None], table, column_table, rows, width
    )
    scattered = (
        jnp.zeros(coefficients.shape, jnp.float32).at[flat_ids].add(returned.reshape(-1, 128))
    )
    update = inverse(scattered, table, column_table, rows, width)
    moved = nesterov * velocity.astype(jnp.float32) + update
    new_velocity = moved.astype(jnp.bfloat16)
    new_param = (param.astype(jnp.float32) - outer_rate * (update + nesterov * moved)).astype(
        jnp.bfloat16
    )
    return (new_error[None], new_param, new_velocity, compressed[None])


def solution(mesh):
    in_specs = (
        P("island", "fsdp", None),
        P("island", "fsdp", None),
        P("fsdp", None),
        P("fsdp", None),
        P("fsdp", None, None),
        P("fsdp", None),
    )
    out_specs = (
        P("island", "fsdp", None),
        P("fsdp", None),
        P("fsdp", None),
        P("fsdp", None, None, None),
    )
    return jax.shard_map(shards, mesh=mesh, in_specs=in_specs, out_specs=out_specs, check_vma=False)
```

profile of v0, /device:TPU:1, one launch (start us, length us, event | category | flops | bytes accessed | tf_op | source)
XLA Modules:
  0.0 191.6 jit_solution(322883646928115541)
XLA Ops:
  7.2 0.8 compare_select_fusion
  8.0 0.1 copy.16
  8.0 0.1 reshape.265
  8.1 0.7 fusion.26
  8.9 0.2 cosine_multiply_fusion.4
  9.1 0.1 copy.12
  9.1 0.1 broadcast_multiply_fusion.1
  9.3 0.1 reshape.288
  9.4 1.3 fusion.6
  10.7 0.2 copy.21
  10.9 1.7 fusion.2
  12.6 1.2 fusion.12
  13.8 1.0 gather_fusion
  14.8 0.8 broadcast_multiply_fusion
  15.7 13.7 %all-to-all-start = ((f32[32,16,128]{2,1,0:T(8,128)}), f32[32,16,128]{2,1,0:T(8,128)S(1)}, u32[]{:S(2)}, u32[]{:S(2)}) async-start(f32[32,16,128]{2,1,0:T(8,128)} %broadcast_multiply_fusion), calls=%async_computation | async-start | bytes 524288 | tf_op jit(solution)/shard_map/all_to_all | solution.py:57
  29.4 0.0 copy-start.6
  29.4 0.0 all-reduce.2.cloned.1.call-start
  29.5 0.1 reshape.275
  29.5 0.6 copy-done.6
  30.1 0.1 copy.14
  30.2 0.1 mul.231
  30.3 0.1 reshape_squeeze.3
  30.4 2.5 %scatter_custom_fusion = f32[2048]{0:T(1024)S(1)} fusion(s32[512]{0:T(512)S(1)} %bitcast.60, f32[512]{0:T(512)S(1)} %reshape.275, f32[]{:T(128)} %constant.13.clone.1), kind=kCustom, calls=%fused_computation.46 | custom fusion | bytes 8196 | tf_op jit(solution)/shard_map/scatter | solution.py:61
  32.9 0.1 mul.237
  32.9 1.3 convolution_bitcast_fusion.1
  34.3 0.6 copy.15
  34.9 5.7 %all-to-all-done = f32[32,16,128]{2,1,0:T(8,128)S(1)} async-done(((f32[32,16,128]{2,1,0:T(8,128)}), f32[32,16,128]{2,1,0:T(8,128)S(1)}, u32[]{:S(2)}, u32[]{:S(2)}) %all-to-all-start) | async-done | bytes 262176 | tf_op jit(solution)/shard_map/all_to_all | solution.py:57
  40.6 0.7 copy-done.3
  41.3 0.0 all-reduce.2.cloned.1.call-update
  41.3 1.0 fusion.32
  42.3 0.2 reshape.256
  42.5 0.0 copy-start
  42.5 110.1 %all-reduce.2.cloned.1.call-done = f32[32,16,128]{2,1,0:T(8,128)} async-done(((f32[32,16,128]{2,1,0:T(8,128)}), f32[32,16,128]{2,1,0:T(8,128)}) %all-reduce.2.cloned.1.call-update) | async-done | bytes 262160 | tf_op jit(solution)/shard_map/psum | solution.py:41
  152.6 1.1 multiply_reduce_fusion
  153.7 1.8 broadcast_divide_fusion
  155.5 9.9 %all-to-all-start.1 = ((f32[32,16,128]{2,1,0:T(8,128)}), f32[32,16,128]{2,1,0:T(8,128)S(1)}, u32[]{:S(2)}, u32[]{:S(2)}) async-start(f32[32,16,128]{2,1,0:T(8,128)} %broadcast_divide_fusion), calls=%async_computation.1 | async-start | bytes 524288 | tf_op jit(solution)/shard_map/all_to_all | solution.py:59
  165.4 1.1 fusion.5
  166.6 0.8 fusion.41
  167.4 9.3 %all-to-all-done.1 = f32[32,16,128]{2,1,0:T(8,128)S(1)} async-done(((f32[32,16,128]{2,1,0:T(8,128)}), f32[32,16,128]{2,1,0:T(8,128)S(1)}, u32[]{:S(2)}, u32[]{:S(2)}) %all-to-all-start.1) | async-done | bytes 262176 | tf_op jit(solution)/shard_map/all_to_all | solution.py:59
  176.7 2.7 %scatter_custom_fusion.1 = f32[2048,128]{1,0:T(8,128)S(1)} fusion(s32[512]{0:T(512)S(1)} %bitcast.61, f32[512,128]{1,0:T(8,128)S(1)} %bitcast.59, f32[]{:T(128)} %constant.13.clone.1), kind=kCustom, calls=%fused_computation.15 | custom fusion | flops 65536 | bytes 1048580 | tf_op jit(solution)/shard_map/scatter-add | solution.py:67
  179.4 1.3 convolution_bitcast_fusion
  180.6 0.6 copy.17
  181.3 1.0 fusion.33
  182.3 0.0 copy-start.4
  182.3 0.2 reshape.261
  182.5 0.8 copy-done.4
  183.3 0.2 copy-done.5
  183.5 1.3 fusion.4
  (13 shorter events, 0.1 us)
Async XLA Ops:
  7.2 2.2 %copy-start.2 = (bf16[1,64,4096]{2,1,0:T(8,128)(2,1)S(1)}, bf16[1,64,4096]{2,1,0:T(8,128)(2,1)}, u32[]{:S(2)}) copy-start(bf16[1,64,4096]{2,1,0:T(8,128)(2,1)} %param.6) | copy-start | bytes 1572868
  15.7 24.9 %all-to-all-start = ((f32[32,16,128]{2,1,0:T(8,128)}), f32[32,16,128]{2,1,0:T(8,128)S(1)}, u32[]{:S(2)}, u32[]{:S(2)}) async-start(f32[32,16,128]{2,1,0:T(8,128)} %broadcast_multiply_fusion), calls=%async_computation | async-start | bytes 524288 | tf_op jit(solution)/shard_map/all_to_all | solution.py:57
  29.4 0.7 copy-start.6
  29.4 123.2 %all-reduce.2.cloned.1.call-start = ((), (), s32[]{:S(2)}) async-start(), calls=%async_computation.2 | async-start | bytes 524288 | tf_op jit(solution)/shard_map/psum | solution.py:41
  40.6 0.7 copy-start.3
  42.5 122.9 %copy-start = (f32[1,64,4096]{2,1,0:T(8,128)S(1)}, f32[1,64,4096]{2,1,0:T(8,128)}, u32[]{:S(2)}) copy-start(f32[1,64,4096]{2,1,0:T(8,128)} %param.7) | copy-start | bytes 3145732
  155.5 21.1 %all-to-all-start.1 = ((f32[32,16,128]{2,1,0:T(8,128)}), f32[32,16,128]{2,1,0:T(8,128)S(1)}, u32[]{:S(2)}, u32[]{:S(2)}) async-start(f32[32,16,128]{2,1,0:T(8,128)} %broadcast_divide_fusion), calls=%async_computation.1 | async-start | bytes 524288 | tf_op jit(solution)/shard_map/all_to_all | solution.py:59
  165.4 1.1 copy-start.1
  182.3 1.0 copy-start.4
  182.3 1.2 copy-start.5
Sparse Core Ops, SparseCore 0:
  41.4 111.1 all-reduce.1
where the time goes:
time: 193 us; the launch traced here: 192 us
  waiting for transfers between devices  125 us (65%)
  starting transfers between devices  23.7 us (12%)
  between operations  14.3 us (7%)
  other arithmetic  12.8 us (7%)
  local copies, waits for them, and re-layouts  8.35 us (4%)
  matrix products  7.44 us (4%)
    psum x1, waiting for transfers between devices, island_norm(): total = lax.psum(pieces, 'island')  110 us
    all_to_all x1, starting transfers between devices, shards(): lax.all_to_all(chosen, 'fsdp', split_axis=0, concat_axis=0, tiled=True)  13.7 us
    all_to_all x1, starting transfers between devices, shards(): lax.all_to_all(compressed, 'fsdp', split_axis=0, concat_axis=0, tiled=True)  9.9 us
    all_to_all x1, waiting for transfers between devices, shards(): lax.all_to_all(compressed, 'fsdp', split_axis=0, concat_axis=0, tiled=True)  9.26 us
    all_to_all x1, waiting for transfers between devices, shards(): lax.all_to_all(chosen, 'fsdp', split_axis=0, concat_axis=0, tiled=True)  5.71 us
  transfers between devices with their start and end apart: 3, of which 3 were waited for; matrix products, arithmetic and copies ran while one was open for 4% of the time, Pallas kernels for 0%

commit v1 on v0

v1 whole, which is shorter than its diff:
```python
import functools
import math

import jax
import jax.numpy as jnp
import ml_dtypes
import numpy as np
from jax import lax
from jax.experimental import pallas as pl
from jax.experimental.pallas import tpu as pltpu
from jax.sharding import PartitionSpec as P

MESH = pl.DeviceIdType.MESH
F32 = jnp.float32
BF16 = jnp.bfloat16

decay_rate = 0.9
outer_rate = 0.7
nesterov = 0.9
eps_value = 1e-06

SIDE = 64
WIDE = 128
FAR_FIRST = (4, 3, 5, 2, 6, 1, 7)


def cosine_table(side):
    freq = np.arange(side, dtype=np.float64)[:, None]
    place = np.arange(side, dtype=np.float64)[None, :]
    scale = np.where(freq == 0, math.sqrt(1.0 / side), math.sqrt(2.0 / side))
    return scale * np.cos(math.pi * (2.0 * place + 1.0) * freq / (2.0 * side))


def halves(table):
    high = table.astype(np.float32).astype(ml_dtypes.bfloat16)
    low = (table - high.astype(np.float64)).astype(ml_dtypes.bfloat16)
    return high, low


def split(values):
    high = values.astype(BF16)
    low = (values - high.astype(F32)).astype(BF16)
    return high, low


def iota(shape, dim):
    return lax.broadcasted_iota(jnp.int32, shape, dim)


def kernel(
    delta, error, param, velocity, ids, counts, rows_fwd, rows_inv, cols_fwd,
    new_error, new_param, new_velocity, compressed,
    ids_s, counts_s, ids_v, counts_v, fwd, inv, cols, d_v, x_v, p_v, v_v, y_v, stack, hot, mask_v, ne_v,
    t_sib, t_own, t_got, part, got, ret, sent, held,
    in_sem, out_sem, sib_sem, rs_send, rs_recv, ag_send, ag_recv, rel_sem, b_send, b_own, b_recv, fin_sem,
    ready_x, ready_y,
):
    i = lax.axis_index("island")
    f = lax.axis_index("fsdp")
    y = lax.div(i, 2)
    core = lax.rem(i, 2)
    z = lax.div(f, 4)
    x = lax.rem(f, 4)
    sibling = (2 * y + (1 - core), f)
    width = error.shape[2]
    step = width // 4
    blocks = step // WIDE

    def y_peer(d):
        return (2 * lax.rem(y + d, 8) + core, f)

    barrier = pltpu.get_barrier_semaphore()
    near = [sibling]
    near += [y_peer(d) for d in range(1, 8)]
    near += [(i, 4 * lax.rem(z + d, 8) + x) for d in range(1, 8)]
    x_line = [(i, 4 * z + lax.rem(x + d, 4)) for d in range(1, 4)]
    near += x_line
    for other in near:
        pl.semaphore_signal(barrier, inc=1, device_id=other, device_id_type=MESH)

    loads = {}

    def load(name, src, dst):
        copy = pltpu.make_async_copy(src, dst, in_sem.at[len(loads)])
        copy.start()
        loads[name] = copy

    load("ids_s", ids.at[0], ids_s)
    load("fwd", rows_fwd, fwd)
    for c in range(4):
        at = pl.ds(c * step, step)
        load(f"e{c}", error.at[0, :, at], x_v.at[:, at])
        load(f"d{c}", delta.at[0, :, at], d_v.at[:, at])
    load("ids_v", ids.at[0], ids_v)
    load("counts_v", counts, counts_v)
    load("counts_s", counts, counts_s)
    load("inv", rows_inv, inv)
    load("cols", cols_fwd, cols)
    load("param", param, p_v)
    load("velocity", velocity, v_v)

    loads["fwd"].wait()
    for c in range(4):
        at = pl.ds(c * step, step)
        loads[f"e{c}"].wait()
        loads[f"d{c}"].wait()
        momentum = decay_rate * x_v[:, at] + d_v[:, at].astype(F32)
        x_v[:, at] = momentum
        high, low = split(momentum)
        stack[0:64, :] = high
        stack[64:128, :] = low
        stack[128:192, :] = high
        field = jnp.dot(fwd[...], stack[...], preferred_element_type=F32)
        for j in range(blocks):
            y_v[pl.ds((c * blocks + j) * SIDE, SIDE), :] = field[:, j * WIDE:(j + 1) * WIDE]

    loads["ids_s"].wait()

    def gather(side, out):
        @pl.loop(0, 32, unroll=4)
        def _(o):
            for k in range(8):
                out[pl.ds(o * 8 + k, 1), :] = y_v[pl.ds(ids_s[o, 8 * side + k], 1), :]

    gather(1 - core, t_sib)
    pl.semaphore_wait(barrier, len(near))
    for other in x_line:
        pl.semaphore_signal(ready_x, inc=1, device_id=other, device_id_type=MESH)
    to_sib = pltpu.make_async_remote_copy(
        src_ref=t_sib, dst_ref=t_got, send_sem=sib_sem.at[0], recv_sem=sib_sem.at[1],
        device_id=sibling, device_id_type=MESH)
    to_sib.start()
    gather(core, t_own)
    to_sib.wait_recv()

    rs = []
    for d in FAR_FIRST + (0,):
        there = lax.rem(y + d, 8)
        at = pl.ds(pl.multiple_of(there * 32, 32), 32)
        part[at, :] = t_own[at, :] + t_got[at, :]
        if d:
            copy = pltpu.make_async_remote_copy(
                src_ref=part.at[at], dst_ref=got.at[d], send_sem=rs_send.at[d], recv_sem=rs_recv.at[d],
                device_id=y_peer(d), device_id_type=MESH)
            copy.start()
            rs.append(copy)

    loads["ids_v"].wait()
    loads["counts_v"].wait()
    loads["inv"].wait()
    eye = iota((32, 32), 0) == iota((32, 32), 1)
    count_column = jnp.sum(jnp.where(eye, counts_v[...].astype(F32), 0.0), axis=1, keepdims=True)
    slot = iota((32, 16), 1).astype(F32)
    listed = jnp.where(slot < count_column, ids_v[...].astype(F32), -1.0)
    entry = iota((16, 512), 1)
    pick = jnp.where(iota((16, 512), 0) == 8 * (entry // 256) + entry % 8, 1.0, 0.0).astype(F32)
    spread = jnp.dot(listed, pick, precision=lax.Precision.HIGHEST, preferred_element_type=F32)
    entry = iota((32, 512), 1)
    spread = jnp.where(iota((32, 512), 0) == (entry // 8) % 32, spread, 0.0)
    place = jnp.sum(spread, axis=0, keepdims=True).astype(jnp.int32)
    row_hot = jnp.where(iota((64, 512), 0) == (place & 63), 1.0, 0.0).astype(BF16)
    block_hot = jnp.where(iota((32, 512), 0) == (place >> 6), 1.0, 0.0).astype(BF16)
    mask_v[...] = lax.dot_general(row_hot, block_hot, (((1,), (1,)), ((), ())), preferred_element_type=F32)

    out_copies = []

    def put(src, dst):
        copy = pltpu.make_async_copy(src, dst, out_sem.at[len(out_copies)])
        copy.start()
        out_copies.append(copy)

    def stack_block(j, values):
        at = pl.ds(j * WIDE, WIDE)
        high, low = split(values)
        stack[0:64, at] = high
        stack[64:128, at] = low
        stack[128:192, at] = high

    def error_part(c):
        at = pl.ds(c * step, step)
        for j in range(blocks):
            q = c * blocks + j
            stack_block(j, y_v[pl.ds(q * SIDE, SIDE), :] * mask_v[:, q:q + 1])
        kept = jnp.dot(inv[...], stack[...], preferred_element_type=F32)
        ne_v[:, at] = x_v[:, at] - kept
        put(ne_v.at[:, at], new_error.at[0, :, at])

    error_part(0)
    error_part(1)
    pl.semaphore_wait(ready_x, 3)
    for d in range(1, 8):
        pl.semaphore_signal(ready_y, inc=1, device_id=y_peer(d), device_id_type=MESH)
    error_part(2)
    error_part(3)

    @pl.loop(0, 32)
    def _(q):
        at = pl.ds(pl.multiple_of(q * SIDE, SIDE), SIDE)
        hot[at, :] = jnp.where(iota((SIDE, 512), 0) + q * SIDE == place, 1.0, 0.0).astype(BF16)

    loads["counts_s"].wait()
    loads["cols"].wait()
    for copy in rs:
        copy.wait_recv()
    mine = pl.ds(pl.multiple_of(y * 32, 32), 32)
    total = part[mine, :]
    for d in range(1, 8):
        total = total + got[d]
    alive = []
    for r in range(4):
        live = iota((8, WIDE), 0) + 8 * core < counts_s[0, 4 * y + r]
        alive.append(jnp.where(live, total[8 * r:8 * r + 8], 0.0))
    total = jnp.concatenate(alive, axis=0)
    normed = total / jnp.sqrt(jnp.mean(total * total, axis=1, keepdims=True) + eps_value)
    ret[core, mine, :] = normed
    ag = []
    for d in FAR_FIRST:
        copy = pltpu.make_async_remote_copy(
            src_ref=ret.at[core, mine], dst_ref=ret.at[core, mine], send_sem=ag_send.at[d], recv_sem=ag_recv.at[d],
            device_id=y_peer(d), device_id_type=MESH)
        copy.start()
        ag.append(copy)
    high, low = split(normed)
    sent[...] = (
        jnp.dot(high, cols[0], preferred_element_type=F32)
        + jnp.dot(low, cols[0], preferred_element_type=F32)
        + jnp.dot(high, cols[1], preferred_element_type=F32)
    )
    pl.semaphore_wait(ready_y, 7)
    owner_sends = []
    for d in FAR_FIRST:
        for r in range(4):
            copy = pltpu.make_async_remote_copy(
                src_ref=sent.at[pl.ds(8 * r, 8)], dst_ref=held.at[f], send_sem=b_send.at[0], recv_sem=b_recv.at[0],
                device_id=(2 * lax.rem(y + d, 8) + core, 4 * y + r), device_id_type=MESH)
            copy.start()
    for r in range(4):
        here = 4 * y + r == f

        @pl.when(here)
        def _():
            pltpu.make_async_copy(sent.at[pl.ds(8 * r, 8)], held.at[f], b_recv.at[0]).start()

        @pl.when(jnp.logical_not(here))
        def _():
            pltpu.make_async_remote_copy(
                src_ref=sent.at[pl.ds(8 * r, 8)], dst_ref=held.at[f], send_sem=b_own.at[r], recv_sem=b_recv.at[0],
                device_id=(i, 4 * y + r), device_id_type=MESH).start()

    for copy in ag:
        copy.wait_recv()
    relay = pltpu.make_async_remote_copy(
        src_ref=ret.at[core], dst_ref=ret.at[core], send_sem=rel_sem.at[0], recv_sem=rel_sem.at[1],
        device_id=sibling, device_id_type=MESH)
    relay.start()
    loads["param"].wait()
    loads["velocity"].wait()
    relay.wait_recv()
    high, low = split(jnp.concatenate([ret[0], ret[1]], axis=0))
    both = jnp.concatenate([high, low], axis=1)
    for c in range(4):
        at = pl.ds(c * step, step)
        pieces = jnp.dot(hot[pl.ds(c * blocks * SIDE, blocks * SIDE), :], both, preferred_element_type=F32)
        for j in range(blocks):
            block = pieces[j * SIDE:(j + 1) * SIDE]
            stack_block(j, block[:, :WIDE] + block[:, WIDE:])
        update = jnp.dot(inv[...], stack[...], preferred_element_type=F32)
        moved = nesterov * v_v[:, at].astype(F32) + update
        p_v[:, at] = (p_v[:, at].astype(F32) - outer_rate * (update + nesterov * moved)).astype(BF16)
        v_v[:, at] = moved.astype(BF16)
        put(v_v.at[:, at], new_velocity.at[:, at])
        put(p_v.at[:, at], new_param.at[:, at])

    pltpu.make_async_copy(held, held, b_recv.at[0]).wait()
    half = compressed.at[0, :, pl.ds(pl.multiple_of(8 * core, 8), 8), :]
    finish = pltpu.make_async_remote_copy(
        src_ref=held, dst_ref=half, send_sem=fin_sem.at[0], recv_sem=fin_sem.at[1],
        device_id=sibling, device_id_type=MESH)
    finish.start()
    put(held, half)
    finish.wait_recv()

    for copy in out_copies:
        copy.wait()
    to_sib.wait_send()
    for copy in rs + ag + [relay, finish]:
        copy.wait_send()
    out_rows = pl.ds(0, 28 * 8)
    pltpu.make_async_copy(part.at[out_rows], part.at[out_rows], b_send.at[0]).wait()
    for r in range(4):
        @pl.when(4 * y + r != f)
        def _():
            pltpu.make_async_remote_copy(
                src_ref=sent.at[pl.ds(8 * r, 8)], dst_ref=held.at[f], send_sem=b_own.at[r], recv_sem=b_recv.at[0],
                device_id=(i, 4 * y + r), device_id_type=MESH).wait_send()


def shards(delta, error, param, velocity, piece_ids, piece_counts):
    table = cosine_table(SIDE)
    high, low = halves(table)
    rows_fwd = jnp.asarray(np.concatenate([high, high, low], axis=1))
    rows_inv = jnp.asarray(np.concatenate([high.T, high.T, low.T], axis=1))
    cols_fwd = jnp.asarray(np.stack(halves(np.kron(np.eye(2), table.T))))
    rows, width = param.shape
    any_space = pl.BlockSpec(memory_space=pl.ANY)
    dma = pltpu.SemaphoreType.DMA
    step = width // 4
    return pl.pallas_call(
        kernel,
        out_shape=(
            jax.ShapeDtypeStruct(error.shape, F32),
            jax.ShapeDtypeStruct(param.shape, BF16),
            jax.ShapeDtypeStruct(param.shape, BF16),
            jax.ShapeDtypeStruct((1, 32, 16, WIDE), F32),
        ),
        in_specs=[any_space] * 9,
        out_specs=(any_space,) * 4,
        scratch_shapes=[
            pltpu.SMEM((32, 16), jnp.int32),
            pltpu.SMEM((1, 32), jnp.int32),
            pltpu.VMEM((32, 16), jnp.int32),
            pltpu.VMEM((1, 32), jnp.int32),
            pltpu.VMEM((64, 192), BF16),
            pltpu.VMEM((64, 192), BF16),
            pltpu.VMEM((2, 128, 128), BF16),
            pltpu.VMEM((rows, width), BF16),
            pltpu.VMEM((rows, width), F32),
            pltpu.VMEM((rows, width), BF16),
            pltpu.VMEM((rows, width), BF16),
            pltpu.VMEM((2048, WIDE), F32),
            pltpu.VMEM((192, step), BF16),
            pltpu.VMEM((2048, 512), BF16),
            pltpu.VMEM((64, 32), F32),
            pltpu.VMEM((rows, width), F32),
            pltpu.VMEM((256, WIDE), F32),
            pltpu.VMEM((256, WIDE), F32),
            pltpu.VMEM((256, WIDE), F32),
            pltpu.VMEM((256, WIDE), F32),
            pltpu.VMEM((8, 32, WIDE), F32),
            pltpu.VMEM((2, 256, WIDE), F32),
            pltpu.VMEM((32, WIDE), F32),
            pltpu.VMEM((32, 8, WIDE), F32),
            dma((20,)),
            dma((16,)),
            dma((2,)),
            dma((8,)),
            dma((8,)),
            dma((8,)),
            dma((8,)),
            dma((2,)),
            dma((1,)),
            dma((4,)),
            dma((1,)),
            dma((2,)),
            pltpu.SemaphoreType.REGULAR,
            pltpu.SemaphoreType.REGULAR,
        ],
        compiler_params=pltpu.CompilerParams(
            collective_id=0, has_side_effects=True, vmem_limit_bytes=56 << 20),
        name="sync",
    )(delta, error, param, velocity, piece_ids, piece_counts, rows_fwd, rows_inv, cols_fwd)


def solution(mesh):
    in_specs = (
        P("island", "fsdp", None),
        P("island", "fsdp", None),
        P("fsdp", None),
        P("fsdp", None),
        P("fsdp", None, None),
        P("fsdp", None),
    )
    out_specs = (
        P("island", "fsdp", None),
        P("fsdp", None),
        P("fsdp", None),
        P("fsdp", None, None, None),
    )
    return jax.shard_map(shards, mesh=mesh, in_specs=in_specs, out_specs=out_specs, check_vma=False)
```

time: 193 us -> 41.4 us (0.21)
  the two profiles are of different devices: /device:TPU:1 before, /device:TPU:9 now
where the time goes in v1:
time: 41.4 us; the launch traced here: 41.1 us
  Pallas kernels  33.7 us (81%)
  local copies, waits for them, and re-layouts  6.73 us (16%)
  between operations  0.65 us (2%)
    pallas_call x1, Pallas kernels, shards(): pl.pallas_call(kernel, out_shape=(jax.ShapeDtypeStruct(error.shape, F32),...  33.7 us
    unnamed x11, local copies, waits for them, and re-layouts  6.73 us

profile of v1, /device:TPU:9, one launch (start us, length us, event | category | flops | bytes accessed | tf_op | source)
XLA Modules:
  0.0 41.1 jit_solution(2037425121687180210)
XLA Ops:
  0.6 1.4 %copy.13.ids = s32[1,32,16]{2,1,0:T(8,128)} copy(s32[1,32,16]{1,2,0:T(8,128)} %param.14) | data formatting | bytes 4096 | tf_op args[4]
  2.0 33.7 %sync.1 = (f32[1,64,4096]{2,1,0:T(8,128)}, bf16[64,4096]{1,0:T(8,128)(2,1)}, bf16[64,4096]{1,0:T(8,128)(2,1)}, f32[1,32,16,128]{3,2,1,0:T(8,128)}) custom-call(bf16[1,64,4096]{2,1,0:T(8,128)(2,1)} %delta.1, f32[1,64,4096]{2,1,0:T(8,128)} %error.1, bf16[64,4096]{1,0:T(8,128)(2,1)} %param.16, bf16[64,4096]{1,0:T(8,128)(2,1)} %velocity.1, ...), custom_call_target="tpu_custom_call" | custom-call | tf_op jit(solution)/shard_map/sync/pallas_call | solution.py:308
  35.7 0.0 copy-start.1
  35.7 2.3 %copy.18 = f32[1,64,4096]{2,1,0:T(8,128)} copy(f32[1,64,4096]{2,1,0:T(8,128)} %get-tuple-element.8) | data formatting | bytes 2097152
  38.0 0.0 copy-done.1
  38.0 0.0 copy-start
  38.0 0.8 %copy.19 = bf16[64,4096]{1,0:T(8,128)(2,1)} copy(bf16[64,4096]{1,0:T(8,128)(2,1)S(1)} %copy-done.1) | data formatting | bytes 1048576
  38.8 0.4 %copy-done = bf16[64,4096]{1,0:T(8,128)(2,1)S(1)} copy-done((bf16[64,4096]{1,0:T(8,128)(2,1)S(1)}, bf16[64,4096]{1,0:T(8,128)(2,1)}, u32[]{:S(2)}) %copy-start) | copy-done | bytes 524312
  39.3 0.0 copy-start.2
  39.3 0.8 %copy.20 = bf16[64,4096]{1,0:T(8,128)(2,1)} copy(bf16[64,4096]{1,0:T(8,128)(2,1)S(1)} %copy-done) | data formatting | bytes 1048576
  40.1 0.3 copy-done.2
  40.4 0.7 %copy.21 = f32[1,32,16,128]{3,2,1,0:T(8,128)} copy(f32[1,32,16,128]{3,2,1,0:T(8,128)S(1)} %copy-done.2) | data formatting | bytes 524288
Async XLA Ops:
  35.7 2.3 %copy-start.1 = (bf16[64,4096]{1,0:T(8,128)(2,1)S(1)}, bf16[64,4096]{1,0:T(8,128)(2,1)}, u32[]{:S(2)}) copy-start(bf16[64,4096]{1,0:T(8,128)(2,1)} %get-tuple-element.9) | copy-start | bytes 1572868
  38.0 1.2 %copy-start = (bf16[64,4096]{1,0:T(8,128)(2,1)S(1)}, bf16[64,4096]{1,0:T(8,128)(2,1)}, u32[]{:S(2)}) copy-start(bf16[64,4096]{1,0:T(8,128)(2,1)} %get-tuple-element.10) | copy-start | bytes 1572868
  39.3 1.1 %copy-start.2 = (f32[1,32,16,128]{3,2,1,0:T(8,128)S(1)}, f32[1,32,16,128]{3,2,1,0:T(8,128)}, u32[]{:S(2)}) copy-start(f32[1,32,16,128]{3,2,1,0:T(8,128)} %get-tuple-element.11) | copy-start | bytes 786436

commit v2 on v1

v2 whole, which is shorter than its diff:
```python
import functools
import math

import jax
import jax.numpy as jnp
import ml_dtypes
import numpy as np
from jax import lax
from jax.experimental import pallas as pl
from jax.experimental.pallas import tpu as pltpu
from jax.sharding import PartitionSpec as P

MESH = pl.DeviceIdType.MESH
F32 = jnp.float32
BF16 = jnp.bfloat16

decay_rate = 0.9
outer_rate = 0.7
nesterov = 0.9
eps_value = 1e-06

SIDE = 64
WIDE = 128
PEERS = 7


def far(n):
    return 4 + (1 - 2 * lax.rem(n, 2)) * lax.div(n + 1, 2)


def cosine_table(side):
    freq = np.arange(side, dtype=np.float64)[:, None]
    place = np.arange(side, dtype=np.float64)[None, :]
    scale = np.where(freq == 0, math.sqrt(1.0 / side), math.sqrt(2.0 / side))
    return scale * np.cos(math.pi * (2.0 * place + 1.0) * freq / (2.0 * side))


def halves(table):
    high = table.astype(np.float32).astype(ml_dtypes.bfloat16)
    low = (table - high.astype(np.float64)).astype(ml_dtypes.bfloat16)
    return high, low


def split(values):
    high = values.astype(BF16)
    low = (values - high.astype(F32)).astype(BF16)
    return high, low


def iota(shape, dim):
    return lax.broadcasted_iota(jnp.int32, shape, dim)


def kernel(
    delta, error, param, velocity, ids, counts, rows_fwd, rows_inv, cols_fwd,
    new_error, new_param, new_velocity, compressed,
    ids_s, counts_s, ids_v, counts_v, fwd, inv, cols, d_v, x_v, p_v, v_v, y_v, stack, hot, mask_v,
    t_sib, t_own, t_got, part, got, ret, sent,
    in_sem, field_sem, sib_sem, rs_send, rs_recv, ag_send, ag_recv, rel_sem, b_send, b_own, b_recv, fin_sem,
    ready_x, ready_y,
):
    i = lax.axis_index("island")
    f = lax.axis_index("fsdp")
    y = lax.div(i, 2)
    core = lax.rem(i, 2)
    z = lax.div(f, 4)
    x = lax.rem(f, 4)
    sibling = (2 * y + (1 - core), f)
    width = error.shape[2]
    step = width // 4
    blocks = step // WIDE

    half = compressed.at[0, :, pl.ds(pl.multiple_of(8 * core, 8), 8), :]

    def share(shard):
        return compressed.at[0, shard, pl.ds(pl.multiple_of(8 * core, 8), 8), :]

    def y_peer(d):
        return (2 * lax.rem(y + d, 8) + core, f)

    barrier = pltpu.get_barrier_semaphore()

    def greet(other):
        pl.semaphore_signal(barrier, inc=1, device_id=other, device_id_type=MESH)

    @pl.loop(0, PEERS)
    def _(n):
        greet(y_peer(far(n)))
        greet((i, 4 * lax.rem(z + far(n), 8) + x))

    @pl.loop(1, 4)
    def _(n):
        greet((i, 4 * z + lax.rem(x + n, 4)))

    greet(sibling)

    loads = {}

    def load(name, src, dst):
        copy = pltpu.make_async_copy(src, dst, in_sem.at[len(loads)])
        copy.start()
        loads[name] = copy

    load("ids_s", ids, ids_s)
    load("fwd", rows_fwd, fwd)

    def columns(c):
        return pl.ds(pl.multiple_of(c * step, step), step)

    def field_loads(c):
        at = columns(c)
        return (
            pltpu.make_async_copy(error.at[0, :, at], x_v.at[:, at], field_sem.at[2 * c]),
            pltpu.make_async_copy(delta.at[0, :, at], d_v.at[:, at], field_sem.at[2 * c + 1]),
        )

    @pl.loop(0, 4)
    def _(c):
        for copy in field_loads(c):
            copy.start()

    load("ids_v", ids, ids_v)
    load("counts_v", counts, counts_v)
    load("counts_s", counts, counts_s)
    load("inv", rows_inv, inv)
    load("cols", cols_fwd, cols)
    load("param", param, p_v)
    load("velocity", velocity, v_v)

    loads["fwd"].wait()

    @pl.loop(0, 4)
    def _(c):
        at = columns(c)
        for copy in field_loads(c):
            copy.wait()
        momentum = decay_rate * x_v[:, at] + d_v[:, at].astype(F32)
        x_v[:, at] = momentum
        high, low = split(momentum)
        stack[0:64, :] = high
        stack[64:128, :] = low
        stack[128:192, :] = high
        field = jnp.dot(fwd[...], stack[...], preferred_element_type=F32)
        for j in range(blocks):
            at = pl.ds(pl.multiple_of((c * blocks + j) * SIDE, SIDE), SIDE)
            y_v[at, :] = field[:, j * WIDE:(j + 1) * WIDE]

    loads["ids_s"].wait()

    def gather(side, out):
        @pl.loop(0, 32)
        def _(o):
            for k in range(8):
                out[pl.ds(o * 8 + k, 1), :] = y_v[pl.ds(ids_s[8 * side + k, o], 1), :]

    gather(1 - core, t_sib)
    pl.semaphore_wait(barrier, 2 * PEERS + 4)

    @pl.loop(1, 4)
    def _(n):
        pl.semaphore_signal(ready_x, inc=1, device_id=(i, 4 * z + lax.rem(x + n, 4)), device_id_type=MESH)

    to_sib = pltpu.make_async_remote_copy(
        src_ref=t_sib, dst_ref=t_got, send_sem=sib_sem.at[0], recv_sem=sib_sem.at[1],
        device_id=sibling, device_id_type=MESH)
    to_sib.start()
    gather(core, t_own)
    to_sib.wait_recv()

    def sums(d):
        at = pl.ds(pl.multiple_of(lax.rem(y + d, 8) * 32, 32), 32)
        return pltpu.make_async_remote_copy(
            src_ref=part.at[at], dst_ref=got.at[d], send_sem=rs_send.at[d], recv_sem=rs_recv.at[d],
            device_id=y_peer(d), device_id_type=MESH)

    @pl.loop(0, PEERS)
    def _(n):
        at = pl.ds(pl.multiple_of(lax.rem(y + far(n), 8) * 32, 32), 32)
        part[at, :] = t_own[at, :] + t_got[at, :]
        sums(far(n)).start()

    mine = pl.ds(pl.multiple_of(y * 32, 32), 32)
    part[mine, :] = t_own[mine, :] + t_got[mine, :]
    pl.semaphore_wait(ready_x, 3)

    @pl.loop(1, 8)
    def _(d):
        pl.semaphore_signal(ready_y, inc=1, device_id=y_peer(d), device_id_type=MESH)

    loads["ids_v"].wait()
    loads["counts_v"].wait()
    loads["inv"].wait()
    listed = jnp.where(iota((16, 32), 0) < counts_v[...], ids_v[...], -1).astype(F32)
    entry = iota((32, 512), 1)
    pick = jnp.where(iota((32, 512), 0) == (entry // 8) % 32, 1.0, 0.0).astype(F32)
    spread = jnp.dot(listed, pick, precision=lax.Precision.HIGHEST, preferred_element_type=F32)
    entry = iota((16, 512), 1)
    spread = jnp.where(iota((16, 512), 0) == 8 * (entry // 256) + entry % 8, spread, 0.0)
    place = jnp.sum(spread, axis=0, keepdims=True).astype(jnp.int32)
    row_hot = jnp.where(iota((64, 512), 0) == (place & 63), 1.0, 0.0).astype(BF16)
    block_hot = jnp.where(iota((32, 512), 0) == (place >> 6), 1.0, 0.0).astype(BF16)
    mask_v[:, 0:32] = lax.dot_general(row_hot, block_hot, (((1,), (1,)), ((), ())), preferred_element_type=F32)

    def stack_block(j, values):
        at = pl.ds(j * WIDE, WIDE)
        high, low = split(values)
        stack[0:64, at] = high
        stack[64:128, at] = low
        stack[128:192, at] = high

    @pl.loop(0, 4)
    def _(c):
        at = columns(c)
        mask = pltpu.roll(mask_v[...], WIDE - c * blocks, 1)
        for j in range(blocks):
            rows = pl.ds(pl.multiple_of((c * blocks + j) * SIDE, SIDE), SIDE)
            stack_block(j, y_v[rows, :] * mask[:, j:j + 1])
        kept = jnp.dot(inv[...], stack[...], preferred_element_type=F32)
        new_error[0, :, at] = x_v[:, at] - kept

    @pl.loop(0, 32)
    def _(q):
        at = pl.ds(pl.multiple_of(q * SIDE, SIDE), SIDE)
        hot[at, :] = jnp.where(iota((SIDE, 512), 0) + q * SIDE == place, 1.0, 0.0).astype(BF16)

    loads["counts_s"].wait()
    loads["cols"].wait()

    @pl.loop(1, 8)
    def _(d):
        sums(d).wait_recv()

    total = part[mine, :]
    for d in range(1, 8):
        total = total + got[d]
    alive = []
    for r in range(4):
        live = iota((8, WIDE), 0) + 8 * core < counts_s[0, 4 * y + r]
        alive.append(jnp.where(live, total[8 * r:8 * r + 8], 0.0))
    total = jnp.concatenate(alive, axis=0)
    normed = total / jnp.sqrt(jnp.mean(total * total, axis=1, keepdims=True) + eps_value)
    ret[core, mine, :] = normed
    high, low = split(normed)
    sent[...] = (
        jnp.dot(high, cols[0], preferred_element_type=F32)
        + jnp.dot(low, cols[0], preferred_element_type=F32)
        + jnp.dot(high, cols[1], preferred_element_type=F32)
    )
    pl.semaphore_wait(ready_y, 7)

    @pl.loop(0, 4 * PEERS)
    def _(n):
        r = lax.rem(n, 4)
        pltpu.make_async_remote_copy(
            src_ref=sent.at[pl.ds(pl.multiple_of(8 * r, 8), 8)], dst_ref=share(f),
            send_sem=b_send.at[0], recv_sem=b_recv.at[0],
            device_id=(2 * lax.rem(y + far(lax.div(n, 4)), 8) + core, 4 * y + r), device_id_type=MESH).start()

    def plane(r):
        return pltpu.make_async_remote_copy(
            src_ref=sent.at[pl.ds(pl.multiple_of(8 * r, 8), 8)], dst_ref=share(f),
            send_sem=b_own.at[r], recv_sem=b_recv.at[0],
            device_id=(i, 4 * y + r), device_id_type=MESH)

    @pl.loop(0, 4)
    def _(r):
        @pl.when(4 * y + r == f)
        def _():
            at = pl.ds(pl.multiple_of(8 * r, 8), 8)
            pltpu.make_async_copy(sent.at[at], share(f), b_recv.at[0]).start()

        @pl.when(4 * y + r != f)
        def _():
            plane(r).start()

    def back(d):
        return pltpu.make_async_remote_copy(
            src_ref=ret.at[core, mine], dst_ref=ret.at[core, mine], send_sem=ag_send.at[d], recv_sem=ag_recv.at[d],
            device_id=y_peer(d), device_id_type=MESH)

    @pl.loop(0, PEERS)
    def _(n):
        back(far(n)).start()


    @pl.loop(1, 8)
    def _(d):
        back(d).wait_recv()

    relay = pltpu.make_async_remote_copy(
        src_ref=ret.at[core], dst_ref=ret.at[core], send_sem=rel_sem.at[0], recv_sem=rel_sem.at[1],
        device_id=sibling, device_id_type=MESH)
    relay.start()
    def spread(side, first):
        high, low = split(ret[side])
        both = jnp.concatenate([high, low], axis=1)
        entries = pl.ds(pl.multiple_of(side * 256, 256), 256)

        @pl.loop(0, 4)
        def _(c):
            rows = pl.ds(pl.multiple_of(c * blocks * SIDE, blocks * SIDE), blocks * SIDE)
            pieces = jnp.dot(hot[rows, entries], both, preferred_element_type=F32)
            pieces = pieces[:, :WIDE] + pieces[:, WIDE:]
            if first:
                y_v[rows, :] = pieces
            else:
                finish_update(c, y_v[rows, :] + pieces)

    def finish_update(c, pieces):
        at = columns(c)
        for j in range(blocks):
            stack_block(j, pieces[j * SIDE:(j + 1) * SIDE])
        update = jnp.dot(inv[...], stack[...], preferred_element_type=F32)
        moved = nesterov * v_v[:, at].astype(F32) + update
        new_param[:, at] = (p_v[:, at].astype(F32) - outer_rate * (update + nesterov * moved)).astype(BF16)
        new_velocity[:, at] = moved.astype(BF16)

    spread(core, True)

    pltpu.make_async_copy(half, half, b_recv.at[0]).wait()
    finish = pltpu.make_async_remote_copy(
        src_ref=half, dst_ref=half, send_sem=fin_sem.at[0], recv_sem=fin_sem.at[1],
        device_id=sibling, device_id_type=MESH)
    finish.start()
    loads["param"].wait()
    loads["velocity"].wait()
    relay.wait_recv()
    spread(1 - core, False)
    finish.wait_recv()

    to_sib.wait_send()
    relay.wait_send()
    finish.wait_send()

    @pl.loop(1, 8)
    def _(d):
        sums(d).wait_send()
        back(d).wait_send()

    out_rows = pl.ds(0, 28 * 8)
    pltpu.make_async_copy(part.at[out_rows], part.at[out_rows], b_send.at[0]).wait()

    @pl.loop(0, 4)
    def _(r):
        @pl.when(4 * y + r != f)
        def _():
            plane(r).wait_send()


def settle(*refs):
    sources, targets, sem = refs[:4], refs[4:8], refs[8]
    copies = [pltpu.make_async_copy(a, b, sem.at[n]) for n, (a, b) in enumerate(zip(sources, targets))]
    for copy in copies:
        copy.start()
    for copy in copies:
        copy.wait()


def shards(delta, error, param, velocity, piece_ids, piece_counts):
    table = cosine_table(SIDE)
    high, low = halves(table)
    rows_fwd = jnp.asarray(np.concatenate([high, high, low], axis=1))
    rows_inv = jnp.asarray(np.concatenate([high.T, high.T, low.T], axis=1))
    cols_fwd = jnp.asarray(np.stack(halves(np.kron(np.eye(2), table.T))))
    rows, width = param.shape
    any_space = pl.BlockSpec(memory_space=pl.ANY)
    dma = pltpu.SemaphoreType.DMA
    step = width // 4
    results = pl.pallas_call(
        kernel,
        out_shape=(
            pltpu.VMEM(error.shape, F32),
            pltpu.VMEM(param.shape, BF16),
            pltpu.VMEM(param.shape, BF16),
            pltpu.VMEM((1, 32, 16, WIDE), F32),
        ),
        in_specs=[any_space] * 9,
        out_specs=(pl.BlockSpec(memory_space=pltpu.VMEM),) * 4,
        scratch_shapes=[
            pltpu.SMEM((16, 32), jnp.int32),
            pltpu.SMEM((1, 32), jnp.int32),
            pltpu.VMEM((16, 32), jnp.int32),
            pltpu.VMEM((1, 32), jnp.int32),
            pltpu.VMEM((64, 192), BF16),
            pltpu.VMEM((64, 192), BF16),
            pltpu.VMEM((2, 128, 128), BF16),
            pltpu.VMEM((rows, width), BF16),
            pltpu.VMEM((rows, width), F32),
            pltpu.VMEM((rows, width), BF16),
            pltpu.VMEM((rows, width), BF16),
            pltpu.VMEM((2048, WIDE), F32),
            pltpu.VMEM((192, step), BF16),
            pltpu.VMEM((2048, 512), BF16),
            pltpu.VMEM((64, 128), F32),
            pltpu.VMEM((256, WIDE), F32),
            pltpu.VMEM((256, WIDE), F32),
            pltpu.VMEM((256, WIDE), F32),
            pltpu.VMEM((256, WIDE), F32),
            pltpu.VMEM((8, 32, WIDE), F32),
            pltpu.VMEM((2, 256, WIDE), F32),
            pltpu.VMEM((32, WIDE), F32),
            dma((20,)),
            dma((8,)),
            dma((2,)),
            dma((8,)),
            dma((8,)),
            dma((8,)),
            dma((8,)),
            dma((2,)),
            dma((1,)),
            dma((4,)),
            dma((1,)),
            dma((2,)),
            pltpu.SemaphoreType.REGULAR,
            pltpu.SemaphoreType.REGULAR,
        ],
        compiler_params=pltpu.CompilerParams(
            collective_id=0, has_side_effects=True, vmem_limit_bytes=56 << 20),
        name="sync",
    )(delta, error, param, velocity, piece_ids[0].T, piece_counts, rows_fwd, rows_inv, cols_fwd)
    results = [pltpu.with_memory_space_constraint(a, pltpu.VMEM) for a in results]
    return pl.pallas_call(
        settle,
        out_shape=tuple(pltpu.HBM(a.shape, a.dtype) for a in results),
        in_specs=[pl.BlockSpec(memory_space=pltpu.VMEM)] * 4,
        out_specs=(pl.BlockSpec(memory_space=pltpu.HBM),) * 4,
        scratch_shapes=[dma((4,))],
        name="settle",
    )(*results)


def solution(mesh):
    in_specs = (
        P("island", "fsdp", None),
        P("island", "fsdp", None),
        P("fsdp", None),
        P("fsdp", None),
        P("fsdp", None, None),
        P("fsdp", None),
    )
    out_specs = (
        P("island", "fsdp", None),
        P("fsdp", None),
        P("fsdp", None),
        P("fsdp", None, None, None),
    )
    return jax.shard_map(shards, mesh=mesh, in_specs=in_specs, out_specs=out_specs, check_vma=False)
```

time: 41.4 us -> 34.8 us (0.84)
  the two profiles are of different devices: /device:TPU:9 before, /device:TPU:1 now
where the time goes in v2:
time: 34.8 us; the launch traced here: 34.7 us
  Pallas kernels  34 us (98%)
  between operations  0.64 us (2%)
    pallas_call x1, Pallas kernels, shards(): pl.pallas_call(kernel, out_shape=(pltpu.VMEM(error.shape, F32), pltpu.VME...  32.6 us
    pallas_call x1, Pallas kernels, shards(): pl.pallas_call(settle, out_shape=tuple((pltpu.HBM(a.shape, a.dtype) for a...  1.43 us

profile of v2, /device:TPU:1, one launch (start us, length us, event | category | flops | bytes accessed | tf_op | source)
XLA Modules:
  0.0 34.7 jit_solution(13250105533892268491)
XLA Ops:
  0.6 32.6 %sync.1 = (f32[1,64,4096]{2,1,0:T(8,128)S(1)}, bf16[64,4096]{1,0:T(8,128)(2,1)S(1)}, bf16[64,4096]{1,0:T(8,128)(2,1)S(1)}, f32[1,32,16,128]{3,2,1,0:T(8,128)S(1)}) custom-call(bf16[1,64,4096]{2,1,0:T(8,128)(2,1)} %delta.1, f32[1,64,4096]{2,1,0:T(8,128)} %error.1, bf16[64,4096]{1,0:T(8,128)(2,1)} %param.16, bf16[64,4096]{1,0:T(8,128)(2,1)} %velocity.1, ...), custom_call_target="tpu_custom_call" | custom-call | tf_op jit(solution)/shard_map/sync/pallas_call | solution.py:369
  33.2 1.4 %settle.1 = (f32[1,64,4096]{2,1,0:T(8,128)}, bf16[64,4096]{1,0:T(8,128)(2,1)}, bf16[64,4096]{1,0:T(8,128)(2,1)}, f32[1,32,16,128]{3,2,1,0:T(8,128)}) custom-call(f32[1,64,4096]{2,1,0:T(8,128)S(1)} %get-tuple-element.8.refs_0_, bf16[64,4096]{1,0:T(8,128)(2,1)S(1)} %get-tuple-element.9.refs_1_, bf16[64,4096]{1,0:T(8,128)(2,1)S(1)} %get-tuple-element.10.refs_2_, ...), custom_call_target="tpu_custom_call" | custom-call | tf_op jit(solution)/shard_map/settle/pallas_call | solution.py:422

commit v3 on v2

--- a/solution.py
+++ b/solution.py
@@ -54,9 +54,9 @@
 def kernel(
     delta, error, param, velocity, ids, counts, rows_fwd, rows_inv, cols_fwd,
     new_error, new_param, new_velocity, compressed,
-    ids_s, counts_s, ids_v, counts_v, fwd, inv, cols, d_v, x_v, p_v, v_v, y_v, stack, hot, mask_v,
+    ids_s, counts_s, ids_v, counts_v, fwd, inv, cols, d_v, x_v, p_v, v_v, y_v, stack, basis_high, basis_low, mask_v, block_v,
     t_sib, t_own, t_got, part, got, ret, sent,
-    in_sem, field_sem, sib_sem, rs_send, rs_recv, ag_send, ag_recv, rel_sem, b_send, b_own, b_recv, fin_sem,
+    in_sem, field_sem, sib_send, sib_recv, rs_send, rs_recv, ag_send, ag_recv, rel_sem, b_send, b_own, b_recv, fin_sem,
     ready_x, ready_y,
 ):
     i = lax.axis_index("island")
@@ -124,8 +124,6 @@
     load("counts_s", counts, counts_s)
     load("inv", rows_inv, inv)
     load("cols", cols_fwd, cols)
-    load("param", param, p_v)
-    load("velocity", velocity, v_v)
 
     loads["fwd"].wait()
 
@@ -147,38 +145,57 @@
 
     loads["ids_s"].wait()
 
-    def gather(side, out):
-        @pl.loop(0, 32)
-        def _(o):
+    def gather(side, out, site):
+        @pl.loop(0, 4)
+        def _(r):
             for k in range(8):
-                out[pl.ds(o * 8 + k, 1), :] = y_v[pl.ds(ids_s[8 * side + k, o], 1), :]
-
-    gather(1 - core, t_sib)
+                row = ids_s[8 * side + k, 4 * site + r]
+                out[pl.ds(site * 32 + r * 8 + k, 1), :] = y_v[pl.ds(row, 1), :]
+
+    def site_of(n):
+        return lax.rem(y + lax.select(n == PEERS, 0, far(n)), 8)
+
+    def rows_of(site):
+        return pl.ds(pl.multiple_of(site * 32, 32), 32)
+
+    def exchange(n):
+        at = rows_of(site_of(n))
+        return pltpu.make_async_remote_copy(
+            src_ref=t_sib.at[at], dst_ref=t_got.at[at], send_sem=sib_send.at[n], recv_sem=sib_recv.at[n],
+            device_id=sibling, device_id_type=MESH)
+
+    @pl.loop(0, 8)
+    def _(n):
+        gather(1 - core, t_sib, site_of(n))
+
     pl.semaphore_wait(barrier, 2 * PEERS + 4)
 
+    @pl.loop(0, 8)
+    def _(n):
+        exchange(n).start()
+
     @pl.loop(1, 4)
     def _(n):
         pl.semaphore_signal(ready_x, inc=1, device_id=(i, 4 * z + lax.rem(x + n, 4)), device_id_type=MESH)
 
-    to_sib = pltpu.make_async_remote_copy(
-        src_ref=t_sib, dst_ref=t_got, send_sem=sib_sem.at[0], recv_sem=sib_sem.at[1],
-        device_id=sibling, device_id_type=MESH)
-    to_sib.start()
-    gather(core, t_own)
-    to_sib.wait_recv()
+    @pl.loop(0, 8)
+    def _(n):
+        gather(core, t_own, site_of(n))
 
     def sums(d):
-        at = pl.ds(pl.multiple_of(lax.rem(y + d, 8) * 32, 32), 32)
+        at = rows_of(lax.rem(y + d, 8))
         return pltpu.make_async_remote_copy(
             src_ref=part.at[at], dst_ref=got.at[d], send_sem=rs_send.at[d], recv_sem=rs_recv.at[d],
             device_id=y_peer(d), device_id_type=MESH)
 
     @pl.loop(0, PEERS)
     def _(n):
-        at = pl.ds(pl.multiple_of(lax.rem(y + far(n), 8) * 32, 32), 32)
+        at = rows_of(site_of(n))
+        exchange(n).wait_recv()
         part[at, :] = t_own[at, :] + t_got[at, :]
         sums(far(n)).start()
 
+    exchange(PEERS).wait_recv()
     mine = pl.ds(pl.multiple_of(y * 32, 32), 32)
     part[mine, :] = t_own[mine, :] + t_got[mine, :]
     pl.semaphore_wait(ready_x, 3)
@@ -186,6 +203,9 @@
     @pl.loop(1, 8)
     def _(d):
         pl.semaphore_signal(ready_y, inc=1, device_id=y_peer(d), device_id_type=MESH)
+
+    load("param", param, p_v)
+    load("velocity", velocity, v_v)
 
     loads["ids_v"].wait()
     loads["counts_v"].wait()
@@ -200,6 +220,16 @@
     row_hot = jnp.where(iota((64, 512), 0) == (place & 63), 1.0, 0.0).astype(BF16)
     block_hot = jnp.where(iota((32, 512), 0) == (place >> 6), 1.0, 0.0).astype(BF16)
     mask_v[:, 0:32] = lax.dot_general(row_hot, block_hot, (((1,), (1,)), ((), ())), preferred_element_type=F32)
+    block_v[...] = block_hot.astype(F32)
+    entry_high = jnp.dot(inv[:, 0:64], row_hot, preferred_element_type=F32)
+    entry_low = jnp.dot(inv[:, 128:192], row_hot, preferred_element_type=F32)
+
+    @pl.loop(0, 32)
+    def _(q):
+        at = pl.ds(pl.multiple_of(q * SIDE, SIDE), SIDE)
+        here = block_v[pl.ds(q, 1), :]
+        basis_high[at, :] = (entry_high * here).astype(BF16)
+        basis_low[at, :] = (entry_low * here).astype(BF16)
 
     def stack_block(j, values):
         at = pl.ds(j * WIDE, WIDE)
@@ -218,11 +248,6 @@
         kept = jnp.dot(inv[...], stack[...], preferred_element_type=F32)
         new_error[0, :, at] = x_v[:, at] - kept
 
-    @pl.loop(0, 32)
-    def _(q):
-        at = pl.ds(pl.multiple_of(q * SIDE, SIDE), SIDE)
-        hot[at, :] = jnp.where(iota((SIDE, 512), 0) + q * SIDE == place, 1.0, 0.0).astype(BF16)
-
     loads["counts_s"].wait()
     loads["cols"].wait()
 
@@ -238,29 +263,31 @@
         live = iota((8, WIDE), 0) + 8 * core < counts_s[0, 4 * y + r]
         alive.append(jnp.where(live, total[8 * r:8 * r + 8], 0.0))
     total = jnp.concatenate(alive, axis=0)
-    normed = total / jnp.sqrt(jnp.mean(total * total, axis=1, keepdims=True) + eps_value)
-    ret[core, mine, :] = normed
-    high, low = split(normed)
-    sent[...] = (
+    high, low = split(total)
+    spectrum = (
         jnp.dot(high, cols[0], preferred_element_type=F32)
         + jnp.dot(low, cols[0], preferred_element_type=F32)
         + jnp.dot(high, cols[1], preferred_element_type=F32)
     )
+    level = jnp.sqrt(jnp.mean(total * total, axis=1, keepdims=True) + eps_value)
+    sent[...] = spectrum / level
+    ret[core, mine, :] = total / level
     pl.semaphore_wait(ready_y, 7)
 
-    @pl.loop(0, 4 * PEERS)
-    def _(n):
-        r = lax.rem(n, 4)
-        pltpu.make_async_remote_copy(
-            src_ref=sent.at[pl.ds(pl.multiple_of(8 * r, 8), 8)], dst_ref=share(f),
-            send_sem=b_send.at[0], recv_sem=b_recv.at[0],
-            device_id=(2 * lax.rem(y + far(lax.div(n, 4)), 8) + core, 4 * y + r), device_id_type=MESH).start()
-
-    def plane(r):
+    def to_owner(site, r, sem):
         return pltpu.make_async_remote_copy(
-            src_ref=sent.at[pl.ds(pl.multiple_of(8 * r, 8), 8)], dst_ref=share(f),
-            send_sem=b_own.at[r], recv_sem=b_recv.at[0],
-            device_id=(i, 4 * y + r), device_id_type=MESH)
+            src_ref=sent.at[pl.ds(pl.multiple_of(8 * r, 8), 8)], dst_ref=share(f), send_sem=sem, recv_sem=b_recv.at[0],
+            device_id=(2 * site + core, 4 * y + r), device_id_type=MESH)
+
+    def back(d):
+        return pltpu.make_async_remote_copy(
+            src_ref=ret.at[core, mine], dst_ref=ret.at[core, mine], send_sem=ag_send.at[d], recv_sem=ag_recv.at[d],
+            device_id=y_peer(d), device_id_type=MESH)
+
+    @pl.loop(0, 4)
+    def _(r):
+        for n in range(PEERS):
+            to_owner(lax.rem(y + (4, 3, 5, 2, 6, 1, 7)[n], 8), r, b_send.at[0]).start()
 
     @pl.loop(0, 4)
     def _(r):
@@ -271,12 +298,7 @@
 
         @pl.when(4 * y + r != f)
         def _():
-            plane(r).start()
-
-    def back(d):
-        return pltpu.make_async_remote_copy(
-            src_ref=ret.at[core, mine], dst_ref=ret.at[core, mine], send_sem=ag_send.at[d], recv_sem=ag_recv.at[d],
-            device_id=y_peer(d), device_id_type=MESH)
+            to_owner(y, r, b_own.at[r]).start()
 
     @pl.loop(0, PEERS)
     def _(n):
@@ -299,21 +321,20 @@
         @pl.loop(0, 4)
         def _(c):
             rows = pl.ds(pl.multiple_of(c * blocks * SIDE, blocks * SIDE), blocks * SIDE)
-            pieces = jnp.dot(hot[rows, entries], both, preferred_element_type=F32)
-            pieces = pieces[:, :WIDE] + pieces[:, WIDE:]
+            fields = jnp.dot(basis_high[rows, entries], both, preferred_element_type=F32)
+            field = fields[:, :WIDE] + fields[:, WIDE:]
+            field = field + jnp.dot(basis_low[rows, entries], high, preferred_element_type=F32)
             if first:
-                y_v[rows, :] = pieces
+                y_v[rows, :] = field
             else:
-                finish_update(c, y_v[rows, :] + pieces)
-
-    def finish_update(c, pieces):
-        at = columns(c)
-        for j in range(blocks):
-            stack_block(j, pieces[j * SIDE:(j + 1) * SIDE])
-        update = jnp.dot(inv[...], stack[...], preferred_element_type=F32)
-        moved = nesterov * v_v[:, at].astype(F32) + update
-        new_param[:, at] = (p_v[:, at].astype(F32) - outer_rate * (update + nesterov * moved)).astype(BF16)
-        new_velocity[:, at] = moved.astype(BF16)
+                field = y_v[rows, :] + field
+                for j in range(blocks):
+                    at = pl.ds(pl.multiple_of((c * blocks + j) * WIDE, WIDE), WIDE)
+                    update = field[j * SIDE:(j + 1) * SIDE]
+                    moved = nesterov * v_v[:, at].astype(F32) + update
+                    step_back = outer_rate * (update + nesterov * moved)
+                    new_param[:, at] = (p_v[:, at].astype(F32) - step_back).astype(BF16)
+                    new_velocity[:, at] = moved.astype(BF16)
 
     spread(core, True)
 
@@ -328,7 +349,11 @@
     spread(1 - core, False)
     finish.wait_recv()
 
-    to_sib.wait_send()
+
+    @pl.loop(0, 8)
+    def _(n):
+        exchange(n).wait_send()
+
     relay.wait_send()
     finish.wait_send()
 
@@ -344,7 +369,7 @@
     def _(r):
         @pl.when(4 * y + r != f)
         def _():
-            plane(r).wait_send()
+            to_owner(y, r, b_own.at[r]).wait_send()
 
 
 def settle(*refs):
@@ -391,7 +416,9 @@
             pltpu.VMEM((2048, WIDE), F32),
             pltpu.VMEM((192, step), BF16),
             pltpu.VMEM((2048, 512), BF16),
+            pltpu.VMEM((2048, 512), BF16),
             pltpu.VMEM((64, 128), F32),
+            pltpu.VMEM((32, 512), F32),
             pltpu.VMEM((256, WIDE), F32),
             pltpu.VMEM((256, WIDE), F32),
             pltpu.VMEM((256, WIDE), F32),
@@ -401,7 +428,8 @@
             pltpu.VMEM((32, WIDE), F32),
             dma((20,)),
             dma((8,)),
-            dma((2,)),
+            dma((8,)),
+            dma((8,)),
             dma((8,)),
             dma((8,)),
             dma((8,)),

time: 34.8 us -> 33.9 us (0.974)
  Pallas kernels: 34 us -> 33.1 us
    pallas_call x1, Pallas kernels: 32.6 us -> 31.7 us  [shards(): pl.pallas_call(kernel, out_shape=(pltpu.VMEM(error.shape, F32), pltpu.VME...]
where the time goes in v3:
time: 33.9 us; the launch traced here: 33.7 us
  Pallas kernels  33.1 us (98%)
  between operations  0.64 us (2%)
    pallas_call x1, Pallas kernels, shards(): pl.pallas_call(kernel, out_shape=(pltpu.VMEM(error.shape, F32), pltpu.VME...  31.7 us
    pallas_call x1, Pallas kernels, shards(): pl.pallas_call(settle, out_shape=tuple((pltpu.HBM(a.shape, a.dtype) for a...  1.43 us

profile of v3, /device:TPU:1, one launch (start us, length us, event | category | flops | bytes accessed | tf_op | source)
XLA Modules:
  0.0 33.7 jit_solution(2301084200464349063)
XLA Ops:
  0.6 31.7 %sync.1 = (f32[1,64,4096]{2,1,0:T(8,128)S(1)}, bf16[64,4096]{1,0:T(8,128)(2,1)S(1)}, bf16[64,4096]{1,0:T(8,128)(2,1)S(1)}, f32[1,32,16,128]{3,2,1,0:T(8,128)S(1)}) custom-call(bf16[1,64,4096]{2,1,0:T(8,128)(2,1)} %delta.1, f32[1,64,4096]{2,1,0:T(8,128)} %error.1, bf16[64,4096]{1,0:T(8,128)(2,1)} %param.16, bf16[64,4096]{1,0:T(8,128)(2,1)} %velocity.1, ...), custom_call_target="tpu_custom_call" | custom-call | tf_op jit(solution)/shard_map/sync/pallas_call | solution.py:394
  32.3 1.4 %settle.1 = (f32[1,64,4096]{2,1,0:T(8,128)}, bf16[64,4096]{1,0:T(8,128)(2,1)}, bf16[64,4096]{1,0:T(8,128)(2,1)}, f32[1,32,16,128]{3,2,1,0:T(8,128)}) custom-call(f32[1,64,4096]{2,1,0:T(8,128)S(1)} %get-tuple-element.8.refs_0_, bf16[64,4096]{1,0:T(8,128)(2,1)S(1)} %get-tuple-element.9.refs_1_, bf16[64,4096]{1,0:T(8,128)(2,1)S(1)} %get-tuple-element.10.refs_2_, ...), custom_call_target="tpu_custom_call" | custom-call | tf_op jit(solution)/shard_map/settle/pallas_call | solution.py:450

commit v4 on v3

--- a/solution.py
+++ b/solution.py
@@ -92,6 +92,8 @@
     def _(n):
         greet((i, 4 * z + lax.rem(x + n, 4)))
 
+    opposite = (2 * lax.rem(y + 4, 8) + 1 - core, f)
+    greet(opposite)
     greet(sibling)
 
     loads = {}
@@ -168,19 +170,27 @@
     def _(n):
         gather(1 - core, t_sib, site_of(n))
 
-    pl.semaphore_wait(barrier, 2 * PEERS + 4)
-
     @pl.loop(0, 8)
     def _(n):
+        gather(core, t_own, site_of(n))
+
+    pl.semaphore_wait(barrier, 2 * PEERS + 5)
+
+    def direct(source, other, slot):
+        return pltpu.make_async_remote_copy(
+            src_ref=source.at[rows_of(site_of(0))], dst_ref=got.at[slot],
+            send_sem=rs_send.at[slot], recv_sem=rs_recv.at[slot], device_id=other, device_id_type=MESH)
+
+    direct(t_own, y_peer(4), 4).start()
+    direct(t_sib, opposite, 0).start()
+
+    @pl.loop(1, 8)
+    def _(n):
         exchange(n).start()
 
     @pl.loop(1, 4)
     def _(n):
         pl.semaphore_signal(ready_x, inc=1, device_id=(i, 4 * z + lax.rem(x + n, 4)), device_id_type=MESH)
-
-    @pl.loop(0, 8)
-    def _(n):
-        gather(core, t_own, site_of(n))
 
     def sums(d):
         at = rows_of(lax.rem(y + d, 8))
@@ -188,7 +198,7 @@
             src_ref=part.at[at], dst_ref=got.at[d], send_sem=rs_send.at[d], recv_sem=rs_recv.at[d],
             device_id=y_peer(d), device_id_type=MESH)
 
-    @pl.loop(0, PEERS)
+    @pl.loop(1, PEERS)
     def _(n):
         at = rows_of(site_of(n))
         exchange(n).wait_recv()
@@ -251,12 +261,12 @@
     loads["counts_s"].wait()
     loads["cols"].wait()
 
-    @pl.loop(1, 8)
+    @pl.loop(0, 8)
     def _(d):
         sums(d).wait_recv()
 
     total = part[mine, :]
-    for d in range(1, 8):
+    for d in range(8):
         total = total + got[d]
     alive = []
     for r in range(4):
@@ -264,14 +274,10 @@
         alive.append(jnp.where(live, total[8 * r:8 * r + 8], 0.0))
     total = jnp.concatenate(alive, axis=0)
     high, low = split(total)
-    spectrum = (
-        jnp.dot(high, cols[0], preferred_element_type=F32)
-        + jnp.dot(low, cols[0], preferred_element_type=F32)
-        + jnp.dot(high, cols[1], preferred_element_type=F32)
-    )
-    level = jnp.sqrt(jnp.mean(total * total, axis=1, keepdims=True) + eps_value)
-    sent[...] = spectrum / level
-    ret[core, mine, :] = total / level
+    spectrum = jnp.dot(jnp.concatenate([high, low, high], axis=1), cols[...], preferred_element_type=F32)
+    scale = 1.0 / jnp.sqrt(jnp.mean(total * total, axis=1, keepdims=True) + eps_value)
+    sent[...] = spectrum * scale
+    ret[core, mine, :] = total * scale
     pl.semaphore_wait(ready_y, 7)
 
     def to_owner(site, r, sem):
@@ -305,14 +311,20 @@
         back(far(n)).start()
 
 
-    @pl.loop(1, 8)
-    def _(d):
+    def relay(d):
+        at = pl.ds(pl.multiple_of(lax.rem(y + 8 - d, 8) * 32, 32), 32)
+        return pltpu.make_async_remote_copy(
+            src_ref=ret.at[core, at], dst_ref=ret.at[core, at], send_sem=rel_sem.at[0], recv_sem=rel_sem.at[1],
+            device_id=sibling, device_id_type=MESH)
+
+    relay(0).start()
+
+    @pl.loop(0, PEERS)
+    def _(n):
+        d = far(PEERS - 1 - n)
         back(d).wait_recv()
-
-    relay = pltpu.make_async_remote_copy(
-        src_ref=ret.at[core], dst_ref=ret.at[core], send_sem=rel_sem.at[0], recv_sem=rel_sem.at[1],
-        device_id=sibling, device_id_type=MESH)
-    relay.start()
+        relay(d).start()
+
     def spread(side, first):
         high, low = split(ret[side])
         both = jnp.concatenate([high, low], axis=1)
@@ -345,16 +357,17 @@
     finish.start()
     loads["param"].wait()
     loads["velocity"].wait()
-    relay.wait_recv()
+    pltpu.make_async_copy(ret.at[core], ret.at[core], rel_sem.at[1]).wait()
     spread(1 - core, False)
     finish.wait_recv()
 
 
-    @pl.loop(0, 8)
+    @pl.loop(1, 8)
     def _(n):
         exchange(n).wait_send()
 
-    relay.wait_send()
+    sums(0).wait_send()
+    pltpu.make_async_copy(ret.at[core], ret.at[core], rel_sem.at[0]).wait()
     finish.wait_send()
 
     @pl.loop(1, 8)
@@ -386,7 +399,8 @@
     high, low = halves(table)
     rows_fwd = jnp.asarray(np.concatenate([high, high, low], axis=1))
     rows_inv = jnp.asarray(np.concatenate([high.T, high.T, low.T], axis=1))
-    cols_fwd = jnp.asarray(np.stack(halves(np.kron(np.eye(2), table.T))))
+    high, low = halves(np.kron(np.eye(2), table.T))
+    cols_fwd = jnp.asarray(np.concatenate([high, high, low], axis=0))
     rows, width = param.shape
     any_space = pl.BlockSpec(memory_space=pl.ANY)
     dma = pltpu.SemaphoreType.DMA
@@ -408,7 +422,7 @@
             pltpu.VMEM((1, 32), jnp.int32),
             pltpu.VMEM((64, 192), BF16),
             pltpu.VMEM((64, 192), BF16),
-            pltpu.VMEM((2, 128, 128), BF16),
+            pltpu.VMEM((384, 128), BF16),
             pltpu.VMEM((rows, width), BF16),
             pltpu.VMEM((rows, width), F32),
             pltpu.VMEM((rows, width), BF16),

time: 33.9 us -> 33.4 us (0.985)
  Pallas kernels: 33.1 us -> 32.6 us
    pallas_call x1, Pallas kernels: 31.7 us -> 31.1 us  [shards(): pl.pallas_call(kernel, out_shape=(pltpu.VMEM(error.shape, F32), pltpu.VME...]
where the time goes in v4:
time: 33.4 us; the launch traced here: 33.2 us
  Pallas kernels  32.6 us (98%)
  between operations  0.64 us (2%)
    pallas_call x1, Pallas kernels, shards(): pl.pallas_call(kernel, out_shape=(pltpu.VMEM(error.shape, F32), pltpu.VME...  31.1 us
    pallas_call x1, Pallas kernels, shards(): pl.pallas_call(settle, out_shape=tuple((pltpu.HBM(a.shape, a.dtype) for a...  1.43 us

profile of v4, /device:TPU:1, one launch (start us, length us, event | category | flops | bytes accessed | tf_op | source)
XLA Modules:
  0.0 33.2 jit_solution(5116675714254300743)
XLA Ops:
  0.6 31.1 %sync.1 = (f32[1,64,4096]{2,1,0:T(8,128)S(1)}, bf16[64,4096]{1,0:T(8,128)(2,1)S(1)}, bf16[64,4096]{1,0:T(8,128)(2,1)S(1)}, f32[1,32,16,128]{3,2,1,0:T(8,128)S(1)}) custom-call(bf16[1,64,4096]{2,1,0:T(8,128)(2,1)} %delta.1, f32[1,64,4096]{2,1,0:T(8,128)} %error.1, bf16[64,4096]{1,0:T(8,128)(2,1)} %param.16, bf16[64,4096]{1,0:T(8,128)(2,1)} %velocity.1, ...), custom_call_target="tpu_custom_call" | custom-call | tf_op jit(solution)/shard_map/sync/pallas_call | solution.py:408
  31.8 1.4 %settle.1 = (f32[1,64,4096]{2,1,0:T(8,128)}, bf16[64,4096]{1,0:T(8,128)(2,1)}, bf16[64,4096]{1,0:T(8,128)(2,1)}, f32[1,32,16,128]{3,2,1,0:T(8,128)}) custom-call(f32[1,64,4096]{2,1,0:T(8,128)S(1)} %get-tuple-element.8.refs_0_, bf16[64,4096]{1,0:T(8,128)(2,1)S(1)} %get-tuple-element.9.refs_1_, bf16[64,4096]{1,0:T(8,128)(2,1)S(1)} %get-tuple-element.10.refs_2_, ...), custom_call_target="tpu_custom_call" | custom-call | tf_op jit(solution)/shard_map/settle/pallas_call | solution.py:464

commit v5 on v4

--- a/solution.py
+++ b/solution.py
@@ -290,6 +290,15 @@
             src_ref=ret.at[core, mine], dst_ref=ret.at[core, mine], send_sem=ag_send.at[d], recv_sem=ag_recv.at[d],
             device_id=y_peer(d), device_id_type=MESH)
 
+    apart = lax.rem(z - y + 8, 8)
+    close = jnp.logical_or(apart <= 0, apart >= 8)
+
+    @pl.when(close)
+    def _():
+        @pl.loop(0, PEERS)
+        def _(n):
+            back(far(n)).start()
+
     @pl.loop(0, 4)
     def _(r):
         for n in range(PEERS):
@@ -306,9 +315,11 @@
         def _():
             to_owner(y, r, b_own.at[r]).start()
 
-    @pl.loop(0, PEERS)
-    def _(n):
-        back(far(n)).start()
+    @pl.when(jnp.logical_not(close))
+    def _():
+        @pl.loop(0, PEERS)
+        def _(n):
+            back(far(n)).start()
 
 
     def relay(d):

time: 33.4 us -> 33.4 us (level)
  no operation moved by 1% of the time
where the time goes in v5:
time: 33.4 us; the launch traced here: 33.2 us
  Pallas kernels  32.6 us (98%)
  between operations  0.64 us (2%)
    pallas_call x1, Pallas kernels, shards(): pl.pallas_call(kernel, out_shape=(pltpu.VMEM(error.shape, F32), pltpu.VME...  31.1 us
    pallas_call x1, Pallas kernels, shards(): pl.pallas_call(settle, out_shape=tuple((pltpu.HBM(a.shape, a.dtype) for a...  1.43 us

profile of v5, /device:TPU:1, one launch (start us, length us, event | category | flops | bytes accessed | tf_op | source)
XLA Modules:
  0.0 33.2 jit_solution(11791459221471942942)
XLA Ops:
  0.6 31.1 %sync.1 = (f32[1,64,4096]{2,1,0:T(8,128)S(1)}, bf16[64,4096]{1,0:T(8,128)(2,1)S(1)}, bf16[64,4096]{1,0:T(8,128)(2,1)S(1)}, f32[1,32,16,128]{3,2,1,0:T(8,128)S(1)}) custom-call(bf16[1,64,4096]{2,1,0:T(8,128)(2,1)} %delta.1, f32[1,64,4096]{2,1,0:T(8,128)} %error.1, bf16[64,4096]{1,0:T(8,128)(2,1)} %param.16, bf16[64,4096]{1,0:T(8,128)(2,1)} %velocity.1, ...), custom_call_target="tpu_custom_call" | custom-call | tf_op jit(solution)/shard_map/sync/pallas_call | solution.py:419
  31.8 1.4 %settle.1 = (f32[1,64,4096]{2,1,0:T(8,128)}, bf16[64,4096]{1,0:T(8,128)(2,1)}, bf16[64,4096]{1,0:T(8,128)(2,1)}, f32[1,32,16,128]{3,2,1,0:T(8,128)}) custom-call(f32[1,64,4096]{2,1,0:T(8,128)S(1)} %get-tuple-element.8.refs_0_, bf16[64,4096]{1,0:T(8,128)(2,1)S(1)} %get-tuple-element.9.refs_1_, bf16[64,4096]{1,0:T(8,128)(2,1)S(1)} %get-tuple-element.10.refs_2_, ...), custom_call_target="tpu_custom_call" | custom-call | tf_op jit(solution)/shard_map/settle/pallas_call | solution.py:475
